TPU v7x, 32 devices: a whole 2x2x4 slice. The times are simulated.
32 devices in a mesh: groups: 2 (over x), loop: 16 (over z, y, core).
Axes of the slice: x: 2, y: 2, z: 4, core: 2. Of those that a mesh axis runs over, the one named last changes fastest.
Arguments:
- queries: bfloat16 [16384, 2560], P(('groups', 'loop')), parts along dimension 0, may hold values from -6 to 6
- cur_keys: bfloat16 [16384, 2560], P(('groups', 'loop')), parts along dimension 0, may hold values from -6 to 6
- cur_values: bfloat16 [16384, 2560], P(('groups', 'loop')), parts along dimension 0, may hold values from -6 to 6
- past_keys: bfloat16 [1536, 16, 2560], P(('groups', 'loop')), parts along dimension 0, may hold values from -6 to 6
- past_values: bfloat16 [1536, 16, 2560], P(('groups', 'loop')), parts along dimension 0, may hold values from -6 to 6
- pattern: int32 [128, 8], P(('groups', 'loop')), parts along dimension 0, may hold values 0 or 1
- read_blocks: int32 [128, 8], P('groups'), parts along dimension 0, may hold values from 0 to 767, as said below
- out_weight: bfloat16 [2560, 5120], P('loop'), may hold values from -2 to 2
Outputs:
- projected: bfloat16 [16384, 5120], P(('groups', 'loop')), parts along dimension 0
There are 2 independent parts, one for each index of `groups`. A program takes and returns all parts, laid end to end along the dimension named above; an argument that names none is the same for every part. Nothing has to cross between parts.
Inputs may be any that keep to these rules, and one draw needn't show every extreme that they name: `read_blocks`: entries are block numbers of past_keys; block g belongs to region g // 48. In every region the lists of its 4 query blocks together name blocks of each region exactly 2 times.
All inputs are finite; a program needn't handle non-finite values. No bound on the sum of `pattern` on one device may be relied on, other than what follows from the above.
Results may differ from a plain program's by a relative error of at most 0.0057.
Values may be sent and summed in bfloat16 or wider, within the bound.
A program may use at most 192 MiB of HBM per device.

v0:
```python
import jax
import jax.numpy as jnp
from jax import lax
from jax.sharding import PartitionSpec as P

HEADS = 20
HD = 128


NEG = -1e30


def from_partner(value, axis, distance):
    mask = 2**distance
    pairs = [(source, source ^ mask) for source in range(lax.axis_size(axis))]
    return lax.ppermute(value, axis, pairs)


def attend(q_part, k_sess, v_sess, allowed, k_local, v_local, k_remote, v_remote, score_scale):
    score_sess = (
        jnp.einsum("bqhd,khd->bhqk", q_part, k_sess, preferred_element_type=jnp.float32)
        * score_scale
    )
    score_sess = jnp.where(allowed[:, None, None, :], score_sess, NEG)
    score_local = (
        jnp.einsum("bqhd,khd->bhqk", q_part, k_local, preferred_element_type=jnp.float32)
        * score_scale
    )
    score_remote = (
        jnp.einsum("bqhd,bkhd->bhqk", q_part, k_remote, preferred_element_type=jnp.float32)
        * score_scale
    )
    row_max = jnp.maximum(
        jnp.maximum(score_sess.max(-1), score_local.max(-1)), score_remote.max(-1)
    )[..., None]
    weight_sess = jnp.exp(score_sess - row_max)
    weight_local = jnp.exp(score_local - row_max)
    weight_remote = jnp.exp(score_remote - row_max)
    row_total = weight_sess.sum(-1) + weight_local.sum(-1) + weight_remote.sum(-1)
    mixed_sum = jnp.einsum(
        "bhqk,khd->bqhd",
        weight_sess.astype(jnp.bfloat16),
        v_sess,
        preferred_element_type=jnp.float32,
    )
    mixed_sum = mixed_sum + jnp.einsum(
        "bhqk,khd->bqhd",
        weight_local.astype(jnp.bfloat16),
        v_local,
        preferred_element_type=jnp.float32,
    )
    mixed_sum = mixed_sum + jnp.einsum(
        "bhqk,bkhd->bqhd",
        weight_remote.astype(jnp.bfloat16),
        v_remote,
        preferred_element_type=jnp.float32,
    )
    result = mixed_sum / jnp.transpose(row_total, (0, 2, 1))[..., None]
    return result.astype(jnp.bfloat16)


def local(queries, cur_keys, cur_values, past_keys, past_values, pattern, read_blocks, out_weight):
    tok_rows, feature_dim = queries.shape
    query_blocks = pattern.shape[0]
    query_len = tok_rows // query_blocks
    past_count = past_keys.shape[0]
    block_len = past_keys.shape[1]
    list_len = read_blocks.shape[1]
    loop_count = lax.axis_size("loop")
    my_index = lax.axis_index("loop")
    parity = my_index % 2
    picks_per = query_blocks * list_len // loop_count
    partner_keys, partner_values = from_partner((cur_keys, cur_values), "loop", 0)
    sess_keys = jnp.concatenate([cur_keys, partner_keys], axis=0)
    sess_values = jnp.concatenate([cur_values, partner_values], axis=0)
    blocks_local = jnp.where(parity == 0, pattern, jnp.roll(pattern, query_blocks, axis=1)) > 0
    own_block = jnp.arange(2 * query_blocks)[None, :] == jnp.arange(query_blocks)[:, None]
    allowed = jnp.repeat(blocks_local | own_block, query_len, axis=1)
    all_lists = read_blocks.reshape(loop_count, query_blocks * list_len)
    owner_order = jnp.argsort(all_lists // past_count, axis=1, stable=True)
    sorted_ids = jnp.take_along_axis(all_lists, owner_order, axis=1).reshape(
        loop_count, loop_count, picks_per
    )
    wanted = (
        lax.dynamic_index_in_dim(sorted_ids, my_index, axis=1, keepdims=False)
        - my_index * past_count
    )
    send_keys = jnp.take(past_keys, wanted.reshape(-1), axis=0).reshape(
        loop_count, picks_per, block_len, feature_dim
    )
    send_values = jnp.take(past_values, wanted.reshape(-1), axis=0).reshape(
        loop_count, picks_per, block_len, feature_dim
    )
    got_keys, got_values = (
        lax.all_to_all(send_keys, "loop", split_axis=0, concat_axis=0, tiled=True),
        lax.all_to_all(send_values, "loop", split_axis=0, concat_axis=0, tiled=True),
    )
    my_order = lax.dynamic_index_in_dim(owner_order, my_index, axis=0, keepdims=False)
    placing = jnp.argsort(my_order)
    remote_keys = jnp.take(
        got_keys.reshape(loop_count * picks_per, block_len, feature_dim), placing, axis=0
    )
    remote_keys = remote_keys.reshape(query_blocks, list_len * block_len, feature_dim)
    remote_values = jnp.take(
        got_values.reshape(loop_count * picks_per, block_len, feature_dim), placing, axis=0
    )
    remote_values = remote_values.reshape(query_blocks, list_len * block_len, feature_dim)
    local_keys = past_keys.reshape(past_count * block_len, feature_dim)
    local_values = past_values.reshape(past_count * block_len, feature_dim)
    group_heads = 4
    group_width = group_heads * HD
    group_count = HEADS // group_heads
    score_scale = HD ** (-0.5)

    def head_group(group_index, attn_acc):
        col_start = group_index * group_width

        def take_cols(values):
            return lax.dynamic_slice_in_dim(values, col_start, group_width, values.ndim - 1)

        q_part = take_cols(queries).reshape(query_blocks, query_len, group_heads, HD)
        k_sess = take_cols(sess_keys).reshape(2 * tok_rows, group_heads, HD)
        v_sess = take_cols(sess_values).reshape(2 * tok_rows, group_heads, HD)
        k_local = take_cols(local_keys).reshape(past_count * block_len, group_heads, HD)
        v_local = take_cols(local_values).reshape(past_count * block_len, group_heads, HD)
        k_remote = take_cols(remote_keys).reshape(
            query_blocks, list_len * block_len, group_heads, HD
        )
        v_remote = take_cols(remote_values).reshape(
            query_blocks, list_len * block_len, group_heads, HD
        )
        result = attend(
            q_part, k_sess, v_sess, allowed, k_local, v_local, k_remote, v_remote, score_scale
        )
        return lax.dynamic_update_slice_in_dim(
            attn_acc, result.reshape(tok_rows, group_width), col_start, 1
        )

    attended = lax.fori_loop(
        0, group_count, head_group, jnp.zeros((tok_rows, feature_dim), jnp.bfloat16)
    )
    return jnp.dot(
        attended,
        lax.all_gather(out_weight, "loop", axis=0, tiled=True),
        preferred_element_type=jnp.float32,
    ).astype(jnp.bfloat16)


def solution(mesh):
    return jax.shard_map(
        local,
        mesh=mesh,
        in_specs=(
            P(("groups", "loop"), None),
            P(("groups", "loop"), None),
            P(("groups", "loop"), None),
            P(("groups", "loop"), None, None),
            P(("groups", "loop"), None, None),
            P(("groups", "loop"), None),
            P("groups", None),
            P("loop", None),
        ),
        out_specs=P(("groups", "loop"), None),
        check_vma=False,
    )
```

profile of v0, /device:TPU:13, one launch (start us, length us, event | category | flops | bytes accessed | tf_op | source)
XLA Modules:
  0.0 440.1 jit_solution(13844707038326149068)
XLA Ops:
  16.2 5.2 %gather_fusion.3 = bf16[32,16,2560]{2,1,0:T(8,128)(2,1)} fusion(bf16[48,16,2560]{2,1,0:T(8,128)(2,1)} %param.18, s32[1024]{0:T(1024)S(1)} %pad_clamp_fusion.1), kind=kCustom, calls=%fused_computation.2.clone | custom fusion | bytes 5243008 | tf_op jit(solution)/shard_map/jit(_take)/gather | solution.py:91
  25.2 93.4 %all_to_all.10 = bf16[16,2,16,2560]{3,2,1,0:T(8,128)(2,1)} all-to-all(bf16[16,2,16,2560]{3,2,1,0:T(8,128)(2,1)S(1)} %bitcast.148), channel_id=1, replica_groups=mesh['groups'=2,'loop'=16] {'loop'}, dimensions={0} | all-to-all | bytes 5242880 | tf_op jit(solution)/shard_map/all_to_all | solution.py:95
  118.6 8.1 %all-to-all-start.1 = ((bf16[16,2,16,2560]{3,2,1,0:T(8,128)(2,1)}), bf16[16,2,16,2560]{3,2,1,0:T(8,128)(2,1)}, u32[]{:S(2)}, u32[]{:S(2)}) async-start(bf16[16,2,16,2560]{3,2,1,0:T(8,128)(2,1)} %bitcast.7), calls=%async_computation.1 | async-start | bytes 5242880 | tf_op jit(solution)/shard_map/all_to_all | solution.py:96
  134.9 5.6 %pad_maximum_fusion = bf16[1024,2560]{0,1:T(8,128)(2,1)} fusion(bf16[512,2560]{0,1:T(8,128)(2,1)} %collective-permute-done, bf16[512,2560]{0,1:T(8,128)(2,1)} %copy.138), kind=kLoop, calls=%fused_computation.55 | loop fusion | flops 10485760 | bytes 10485760 | tf_op jit(solution)/shard_map/concatenate | solution.py:75
  140.5 4.8 %pad_maximum_fusion.1 = bf16[1024,2560]{0,1:T(8,128)(2,1)} fusion(bf16[512,2560]{0,1:T(8,128)(2,1)} %collective-permute-done.1, bf16[512,2560]{0,1:T(8,128)(2,1)S(1)} %copy.140), kind=kLoop, calls=%fused_computation.56 | loop fusion | flops 10485760 | bytes 10485760 | tf_op jit(solution)/shard_map/concatenate | solution.py:74
  147.7 66.3 %all-to-all-done.1 = bf16[16,2,16,2560]{3,2,1,0:T(8,128)(2,1)} async-done(((bf16[16,2,16,2560]{3,2,1,0:T(8,128)(2,1)}), bf16[16,2,16,2560]{3,2,1,0:T(8,128)(2,1)}, u32[]{:S(2)}, u32[]{:S(2)}) %all-to-all-start.1) | async-done | bytes 2621472 | tf_op jit(solution)/shard_map/all_to_all | solution.py:96
  214.0 3.9 gather_fusion.4
  217.9 4.6 %broadcast_select_fusion = (bf16[32,16,2560]{2,1,0:T(8,128)(2,1)}, bf16[32,16,2560]{2,1,0:T(8,128)(2,1)}) fusion(bf16[32,16,2560]{2,1,0:T(8,128)(2,1)} %gather_fusion.4, pred[32]{0:T(512)(128)(4,1)S(1)} %compare_and_fusion, bf16[32,16,2560]{2,1,0:T(8,128)(2,1)S(1)} %gather_fusion.2), kind=kLoop, calls=%fused_computation.57 | loop fusion | flops 2621440 | bytes 10485792 | tf_op jit(solution)/shard_map/jit(_take)/select_n | solution.py:104
  224.2 188.2 %while.14 = (s32[]{:T(128)}, bf16[512,2560]{1,0:T(8,128)(2,1)}, bf16[1024,2560]{0,1:T(8,128)(2,1)}, bf16[1024,2560]{0,1:T(8,128)(2,1)}, bf16[512,2560]{1,0:T(8,1...) while((s32[]{:T(128)}, bf16[512,2560]{1,0:T(8,128)(2,1)}, ...), condition=%wide.region_9.12_spmd.clone, body=%wide.region_2.11_spmd.clone.sunk | while | flops 2051272704 | bytes 81469688 | solution.py:139
  228.3 4.5 %fusion.77 = (f32[4,4,128]{2,0,1:T(4,128)S(1)}, f32[4,1024,4,128]{3,1,2,0:T(8,128)}) fusion(pred[4,1024]{1,0:T(4,128)(4,1)S(1)} %bitcast.149, bf16[1024,4,128,1]{0,2,3,1:T(8,128)(2,1)S(1)} %bitcast.136, bf16[4,128,4,128]{3,2,1,0:T(4,128)(2,1)S(1)} %reshape.207), kind=kOutput, calls=%fused_computation.10.clone.1 | convolution fusion | flops 543160320 | bytes 9973760 | tf_op jit(solution)/shard_map/while/body/eval_jaxpr/bqhd,khd->bhqk/dot_general | solution.py:21
  240.4 4.0 fusion.82
  244.3 4.6 %fusion.81 = f32[4,4,128]{2,0,1:T(4,128)S(1)} fusion(f32[4,1024,4,128]{3,1,2,0:T(8,128)} %get-tuple-element.378, f32[4,4,128]{2,0,1:T(4,128)S(1)} %copy_maximum_fusion.2, pred[4,1024]{1,0:T(4,128)(4,1)S(1)} %bitcast.150), kind=kLoop, calls=%fused_computation.8.clone.1 | loop fusion | flops 8386560 | bytes 8409088 | tf_op jit(solution)/shard_map/while/body/eval_jaxpr/reduce_sum | solution.py:39
  249.4 4.3 fusion.78
  253.7 5.5 %fusion.79 = f32[4,128,4,128]{1,3,0,2:T(8,128)} fusion(f32[4,128,4,128]{3,1,2,0:T(8,128)S(1)} %fusion.78, bf16[1024,4,128,1]{0,2,3,1:T(8,128)(2,1)S(1)} %bitcast.141, f32[4,1024,4,128]{3,1,2,0:T(8,128)} %get-tuple-element.378, f32[4,4,128]{2,0,1:T(4,128)S(1)} %copy_maximum_fusion.2, pred[4,1024]{1,0:T(4,128)(4,1)S(1)} %bitcast.151), kind=kOutput, calls=%fused_computation.26.clone.1 | convolution fusion | flops 545521664 | bytes 11546624 | tf_op jit(solution)/shard_map/while/body/eval_jaxpr/bhqk,khd->bqhd/dot_general | solution.py:40
  266.3 4.5 %fusion.77 = (f32[4,4,128]{2,0,1:T(4,128)S(1)}, f32[4,1024,4,128]{3,1,2,0:T(8,128)}) fusion(pred[4,1024]{1,0:T(4,128)(4,1)S(1)} %bitcast.149, bf16[1024,4,128,1]{0,2,3,1:T(8,128)(2,1)S(1)} %bitcast.136, bf16[4,128,4,128]{3,2,1,0:T(4,128)(2,1)S(1)} %reshape.207), kind=kOutput, calls=%fused_computation.10.clone.1 | convolution fusion | flops 543160320 | bytes 9973760 | tf_op jit(solution)/shard_map/while/body/eval_jaxpr/bqhd,khd->bhqk/dot_general | solution.py:21
  282.2 4.4 %fusion.81 = f32[4,4,128]{2,0,1:T(4,128)S(1)} fusion(f32[4,1024,4,128]{3,1,2,0:T(8,128)} %get-tuple-element.378, f32[4,4,128]{2,0,1:T(4,128)S(1)} %copy_maximum_fusion.2, pred[4,1024]{1,0:T(4,128)(4,1)S(1)} %bitcast.150), kind=kLoop, calls=%fused_computation.8.clone.1 | loop fusion | flops 8386560 | bytes 8409088 | tf_op jit(solution)/shard_map/while/body/eval_jaxpr/reduce_sum | solution.py:39
  287.1 4.2 fusion.78
  291.3 5.5 %fusion.79 = f32[4,128,4,128]{1,3,0,2:T(8,128)} fusion(f32[4,128,4,128]{3,1,2,0:T(8,128)S(1)} %fusion.78, bf16[1024,4,128,1]{0,2,3,1:T(8,128)(2,1)S(1)} %bitcast.141, f32[4,1024,4,128]{3,1,2,0:T(8,128)} %get-tuple-element.378, f32[4,4,128]{2,0,1:T(4,128)S(1)} %copy_maximum_fusion.2, pred[4,1024]{1,0:T(4,128)(4,1)S(1)} %bitcast.151), kind=kOutput, calls=%fused_computation.26.clone.1 | convolution fusion | flops 545521664 | bytes 11546624 | tf_op jit(solution)/shard_map/while/body/eval_jaxpr/bhqk,khd->bqhd/dot_general | solution.py:40
  303.8 4.5 %fusion.77 = (f32[4,4,128]{2,0,1:T(4,128)S(1)}, f32[4,1024,4,128]{3,1,2,0:T(8,128)}) fusion(pred[4,1024]{1,0:T(4,128)(4,1)S(1)} %bitcast.149, bf16[1024,4,128,1]{0,2,3,1:T(8,128)(2,1)S(1)} %bitcast.136, bf16[4,128,4,128]{3,2,1,0:T(4,128)(2,1)S(1)} %reshape.207), kind=kOutput, calls=%fused_computation.10.clone.1 | convolution fusion | flops 543160320 | bytes 9973760 | tf_op jit(solution)/shard_map/while/body/eval_jaxpr/bqhd,khd->bhqk/dot_general | solution.py:21
  319.7 4.4 %fusion.81 = f32[4,4,128]{2,0,1:T(4,128)S(1)} fusion(f32[4,1024,4,128]{3,1,2,0:T(8,128)} %get-tuple-element.378, f32[4,4,128]{2,0,1:T(4,128)S(1)} %copy_maximum_fusion.2, pred[4,1024]{1,0:T(4,128)(4,1)S(1)} %bitcast.150), kind=kLoop, calls=%fused_computation.8.clone.1 | loop fusion | flops 8386560 | bytes 8409088 | tf_op jit(solution)/shard_map/while/body/eval_jaxpr/reduce_sum | solution.py:39
  324.6 4.2 fusion.78
  328.8 5.5 %fusion.79 = f32[4,128,4,128]{1,3,0,2:T(8,128)} fusion(f32[4,128,4,128]{3,1,2,0:T(8,128)S(1)} %fusion.78, bf16[1024,4,128,1]{0,2,3,1:T(8,128)(2,1)S(1)} %bitcast.141, f32[4,1024,4,128]{3,1,2,0:T(8,128)} %get-tuple-element.378, f32[4,4,128]{2,0,1:T(4,128)S(1)} %copy_maximum_fusion.2, pred[4,1024]{1,0:T(4,128)(4,1)S(1)} %bitcast.151), kind=kOutput, calls=%fused_computation.26.clone.1 | convolution fusion | flops 545521664 | bytes 11546624 | tf_op jit(solution)/shard_map/while/body/eval_jaxpr/bhqk,khd->bqhd/dot_general | solution.py:40
  341.3 4.5 %fusion.77 = (f32[4,4,128]{2,0,1:T(4,128)S(1)}, f32[4,1024,4,128]{3,1,2,0:T(8,128)}) fusion(pred[4,1024]{1,0:T(4,128)(4,1)S(1)} %bitcast.149, bf16[1024,4,128,1]{0,2,3,1:T(8,128)(2,1)S(1)} %bitcast.136, bf16[4,128,4,128]{3,2,1,0:T(4,128)(2,1)S(1)} %reshape.207), kind=kOutput, calls=%fused_computation.10.clone.1 | convolution fusion | flops 543160320 | bytes 9973760 | tf_op jit(solution)/shard_map/while/body/eval_jaxpr/bqhd,khd->bhqk/dot_general | solution.py:21
  353.4 3.8 fusion.82
  357.2 4.4 %fusion.81 = f32[4,4,128]{2,0,1:T(4,128)S(1)} fusion(f32[4,1024,4,128]{3,1,2,0:T(8,128)} %get-tuple-element.378, f32[4,4,128]{2,0,1:T(4,128)S(1)} %copy_maximum_fusion.2, pred[4,1024]{1,0:T(4,128)(4,1)S(1)} %bitcast.150), kind=kLoop, calls=%fused_computation.8.clone.1 | loop fusion | flops 8386560 | bytes 8409088 | tf_op jit(solution)/shard_map/while/body/eval_jaxpr/reduce_sum | solution.py:39
  362.2 4.2 fusion.78
  366.4 5.5 %fusion.79 = f32[4,128,4,128]{1,3,0,2:T(8,128)} fusion(f32[4,128,4,128]{3,1,2,0:T(8,128)S(1)} %fusion.78, bf16[1024,4,128,1]{0,2,3,1:T(8,128)(2,1)S(1)} %bitcast.141, f32[4,1024,4,128]{3,1,2,0:T(8,128)} %get-tuple-element.378, f32[4,4,128]{2,0,1:T(4,128)S(1)} %copy_maximum_fusion.2, pred[4,1024]{1,0:T(4,128)(4,1)S(1)} %bitcast.151), kind=kOutput, calls=%fused_computation.26.clone.1 | convolution fusion | flops 545521664 | bytes 11546624 | tf_op jit(solution)/shard_map/while/body/eval_jaxpr/bhqk,khd->bqhd/dot_general | solution.py:40
  378.8 4.5 %fusion.77 = (f32[4,4,128]{2,0,1:T(4,128)S(1)}, f32[4,1024,4,128]{3,1,2,0:T(8,128)}) fusion(pred[4,1024]{1,0:T(4,128)(4,1)S(1)} %bitcast.149, bf16[1024,4,128,1]{0,2,3,1:T(8,128)(2,1)S(1)} %bitcast.136, bf16[4,128,4,128]{3,2,1,0:T(4,128)(2,1)S(1)} %reshape.207), kind=kOutput, calls=%fused_computation.10.clone.1 | convolution fusion | flops 543160320 | bytes 9973760 | tf_op jit(solution)/shard_map/while/body/eval_jaxpr/bqhd,khd->bhqk/dot_general | solution.py:21
  394.7 4.4 %fusion.81 = f32[4,4,128]{2,0,1:T(4,128)S(1)} fusion(f32[4,1024,4,128]{3,1,2,0:T(8,128)} %get-tuple-element.378, f32[4,4,128]{2,0,1:T(4,128)S(1)} %copy_maximum_fusion.2, pred[4,1024]{1,0:T(4,128)(4,1)S(1)} %bitcast.150), kind=kLoop, calls=%fused_computation.8.clone.1 | loop fusion | flops 8386560 | bytes 8409088 | tf_op jit(solution)/shard_map/while/body/eval_jaxpr/reduce_sum | solution.py:39
  399.7 4.2 fusion.78
  403.9 5.5 %fusion.79 = f32[4,128,4,128]{1,3,0,2:T(8,128)} fusion(f32[4,128,4,128]{3,1,2,0:T(8,128)S(1)} %fusion.78, bf16[1024,4,128,1]{0,2,3,1:T(8,128)(2,1)S(1)} %bitcast.141, f32[4,1024,4,128]{3,1,2,0:T(8,128)} %get-tuple-element.378, f32[4,4,128]{2,0,1:T(4,128)S(1)} %copy_maximum_fusion.2, pred[4,1024]{1,0:T(4,128)(4,1)S(1)} %bitcast.151), kind=kOutput, calls=%fused_computation.26.clone.1 | convolution fusion | flops 545521664 | bytes 11546624 | tf_op jit(solution)/shard_map/while/body/eval_jaxpr/bhqk,khd->bqhd/dot_general | solution.py:40
  412.4 20.8 %convolution_convert_fusion = bf16[512,5120]{1,0:T(8,128)(2,1)} fusion(bf16[512,2560]{1,0:T(8,128)(2,1)} %get-tuple-element.180, bf16[2560,5120]{1,0:T(8,128)(2,1)} %all-gather.2.cloned.1.call-done), kind=kOutput, calls=%fused_computation.54 | convolution fusion | flops 13424394240 | bytes 34078720 | tf_op jit(solution)/shard_map/dot_general | solution.py:142
  (157 shorter events, 112.3 us)
Async XLA Ops:
  6.5 405.9 %all-gather.2.cloned.1.call-start = ((), (), s32[]{:S(2)}) async-start(), calls=%async_computation.2 | async-start | bytes 27852800 | tf_op jit(solution)/shard_map/all_gather | solution.py:144
  118.6 8.1 %copy-start.1 = (bf16[512,2560]{1,0:T(8,128)(2,1)S(1)}, bf16[512,2560]{1,0:T(8,128)(2,1)}, u32[]{:S(2)}) copy-start(bf16[512,2560]{1,0:T(8,128)(2,1)} %param.16) | copy-start | bytes 7864324
  118.6 95.4 %all-to-all-start.1 = ((bf16[16,2,16,2560]{3,2,1,0:T(8,128)(2,1)}), bf16[16,2,16,2560]{3,2,1,0:T(8,128)(2,1)}, u32[]{:S(2)}, u32[]{:S(2)}) async-start(bf16[16,2,16,2560]{3,2,1,0:T(8,128)(2,1)} %bitcast.7), calls=%async_computation.1 | async-start | bytes 5242880 | tf_op jit(solution)/shard_map/all_to_all | solution.py:96
  129.3 5.4 %copy-start.2 = (s32[4,8]{1,0:T(4,128)S(1)}, s32[4,8]{1,0:T(4,128)}, u32[]{:S(2)}) copy-start(s32[4,8]{1,0:T(4,128)} %param.19) | copy-start | bytes 388
  129.3 5.6 %collective-permute-start = (bf16[512,2560]{0,1:T(8,128)(2,1)}, bf16[512,2560]{0,1:T(8,128)(2,1)}, u32[]{:S(2)}, u32[]{:S(2)}) collective-permute-start(bf16[512,2560]{0,1:T(8,128)(2,1)} %copy.138), channel_id=1, source_target_pairs={{0,1},{1,0},{2,3},{3,2},{4,5},{5,4},{6,7},{7,6},{8,9},{9,8},{10,11... | collective-permute-start | bytes 7864328 | tf_op jit(solution)/shard_map/ppermute | solution.py:16
  132.7 7.8 %collective-permute-start.1 = (bf16[512,2560]{0,1:T(8,128)(2,1)S(1)}, bf16[512,2560]{0,1:T(8,128)(2,1)}, u32[]{:S(2)}, u32[]{:S(2)}) collective-permute-start(bf16[512,2560]{0,1:T(8,128)(2,1)S(1)} %copy.140), channel_id=1, source_target_pairs={{0,1},{1,0},{2,3},{3,2},{4,5},{5,4},{6,7},{7,6},{8,9},{9,8},{10,11... | collective-permute-start | bytes 7864328 | tf_op jit(solution)/shard_map/ppermute | solution.py:16
  249.4 4.3 copy-start
  287.1 4.2 copy-start
  324.6 4.2 copy-start
  362.2 4.2 copy-start
  399.7 4.2 copy-start
Sparse Core Ops, SparseCore 0:
  9.0 247.1 all-gather.1
where the time goes:
time: 444 us; the launch traced here: 440 us
  matrix products  120 us (27%)
  blocking collectives  93.4 us (21%)
  local copies, waits for them, and re-layouts  72.6 us (16%)
  waiting for transfers between devices  67 us (15%)
  other arithmetic  64.1 us (14%)
  between operations  13.5 us (3%)
  starting transfers between devices  8.67 us (2%)
    all_to_all x1, blocking collectives, local(): lax.all_to_all(send_keys, 'loop', split_axis=0, concat_axis=0, tiled=True)  93.4 us
    all_to_all x1, waiting for transfers between devices, local(): lax.all_to_all(send_values, 'loop', split_axis=0, concat_axis=0, tiled=True)  66.3 us
    dynamic_slice x40, local copies, waits for them, and re-layouts, take_cols(): lax.dynamic_slice_in_dim(values, col_start, group_width, values.ndim - 1)  38.3 us
    dot_general x5, matrix products, attend(): jnp.einsum('bhqk,khd->bqhd', weight_sess.astype(jnp.bfloat16), v_sess, pr...  27.5 us
    dot_general x5, matrix products, attend(): jnp.einsum('bqhd,khd->bhqk', q_part, k_sess, preferred_element_type=jnp.f...  22.5 us
    reduce_sum x5, other arithmetic, attend(): weight_sess.sum(-1) + weight_local.sum(-1) + weight_remote.sum(-1)  22.3 us
    dot_general x5, matrix products, attend(): jnp.einsum('bhqk,khd->bqhd', weight_local.astype(jnp.bfloat16), v_local,...  21 us
    dot_general x1, matrix products, local(): jnp.dot(attended, lax.all_gather(out_weight, 'loop', axis=0, tiled=True),...  20.8 us
  transfers between devices with their start and end apart: 4, of which 1 were waited for; matrix products, arithmetic and copies ran while one was open for 54% of the time, Pallas kernels for 0%

commit v1 on v0

v1 whole, which is shorter than its diff:
```python
import functools
import math

import jax
import jax.numpy as jnp
from jax import lax
from jax.experimental import pallas as pl
from jax.experimental.pallas import tpu as pltpu
from jax.sharding import PartitionSpec as P

HD = 128
NEG = -1e30
ROWS = 256
FACTOR = HD**-0.5 * math.log2(math.e)
MESH = pl.DeviceIdType.MESH
F32 = jnp.float32
BF16 = jnp.bfloat16


def scores_of(q, k):
    return lax.dot_general(q, k, (((1,), (1,)), ((), ())), preferred_element_type=F32)


def with_ones(v):
    return jnp.concatenate([v, jnp.ones_like(v)], axis=1)


def row_bias(bias, first, count, length):
    rows = [
        jnp.broadcast_to(bias[first + i : first + i + 1, :], (length, bias.shape[1]))
        for i in range(count)
    ]
    return jnp.concatenate(rows, axis=0)


def pick_kernel(n, picks, wanted, pk, pv, send, sem):
    def copies(i):
        reader, pick = i // picks, i % picks
        block = wanted[i]
        return (
            pltpu.make_async_copy(pk.at[block], send.at[reader, 0, pick], sem.at[2 * i]),
            pltpu.make_async_copy(pv.at[block], send.at[reader, 1, pick], sem.at[2 * i + 1]),
        )

    @pl.loop(0, n * picks)
    def _(i):
        for c in copies(i):
            c.start()

    @pl.loop(0, n * picks)
    def _(i):
        for c in copies(i):
            c.wait()


def pick_blocks(wanted, pk, pv, n, picks):
    return pl.pallas_call(
        functools.partial(pick_kernel, n, picks),
        out_shape=jax.ShapeDtypeStruct((n, 2, picks) + pk.shape[1:], pk.dtype),
        in_specs=[
            pl.BlockSpec(memory_space=pltpu.SMEM),
            pl.BlockSpec(memory_space=pl.ANY),
            pl.BlockSpec(memory_space=pl.ANY),
        ],
        out_specs=pl.BlockSpec(memory_space=pl.ANY),
        scratch_shapes=[pltpu.SemaphoreType.DMA((2 * n * picks,))],
        name="pick",
    )(wanted, pk, pv)


def near_kernel(
    n, q, ck, cv, pk, pv, bias, ck_all, cv_all, send,
    acc, mx, tot, got, part, s_sem, r_sem, p_send, p_recv, own_sem,
):
    head = pl.program_id(0)
    me = lax.axis_index("loop")
    partner = me + 1 - 2 * lax.rem(me, 2)

    def to(dst):
        return pltpu.make_async_remote_copy(
            src_ref=send.at[dst], dst_ref=got.at[me], send_sem=s_sem.at[dst],
            recv_sem=r_sem.at[me], device_id={"loop": dst}, device_id_type=MESH,
        )

    def source(src):
        return pltpu.make_async_remote_copy(
            src_ref=send.at[src], dst_ref=got.at[src], send_sem=s_sem.at[src],
            recv_sem=r_sem.at[src], device_id={"loop": src}, device_id_type=MESH,
        )

    def half(i, ref):
        return pltpu.make_async_remote_copy(
            src_ref=ref, dst_ref=part.at[i], send_sem=p_send.at[i],
            recv_sem=p_recv.at[i], device_id={"loop": partner}, device_id_type=MESH,
        )

    own = pltpu.make_async_copy(send.at[me], got.at[me], own_sem)

    @pl.when(head == 0)
    def _():
        barrier = pltpu.get_barrier_semaphore()

        @pl.loop(1, n)
        def _(k):
            pl.semaphore_signal(
                barrier, inc=1, device_id={"loop": lax.rem(me + k, n)}, device_id_type=MESH
            )

        pl.semaphore_wait(barrier, n - 1)

        @pl.loop(1, n)
        def _(k):
            to(lax.rem(me + k, n)).start()

        half(0, ck_all).start()
        half(1, cv_all).start()
        own.start()

    tokens = q.shape[0]
    length = tokens // bias.shape[0]
    v_own, v_past = with_ones(cv[...]), with_ones(pv[...])
    for r in range(0, tokens, ROWS):
        qr = q[r : r + ROWS, :]
        s_own = scores_of(qr, ck[...]) + row_bias(bias, r // length, ROWS // length, length)
        s_past = scores_of(qr, pk[...])
        m = jnp.maximum(s_own.max(-1, keepdims=True), s_past.max(-1, keepdims=True)) * FACTOR
        w_own = jnp.exp2(s_own * FACTOR - m).astype(BF16)
        w_past = jnp.exp2(s_past * FACTOR - m).astype(BF16)
        out = jnp.dot(w_own, v_own, preferred_element_type=F32)
        out = out + jnp.dot(w_past, v_past, preferred_element_type=F32)
        acc[r : r + ROWS, :] = out[:, :HD]
        tot[r : r + ROWS, :] = out[:, HD:]
        mx[r : r + ROWS, :] = jnp.broadcast_to(m, (ROWS, HD))

    @pl.when(head == pl.num_programs(0) - 1)
    def _():
        @pl.loop(1, n)
        def _(k):
            to(lax.rem(me + k, n)).wait_send()
            source(lax.rem(me + k, n)).wait_recv()

        half(0, ck_all).wait()
        half(1, cv_all).wait()
        own.wait()


def near(q, ck, cv, pk, pv, bias, send, n):
    tokens, width = q.shape
    past = pk.shape[0]
    heads = width // HD

    def col(rows):
        return pl.BlockSpec((rows, HD), lambda h: (0, h))

    hbm = pl.BlockSpec(memory_space=pl.ANY)
    f32 = jax.ShapeDtypeStruct((tokens, width), F32)
    dma = pltpu.SemaphoreType.DMA
    return pl.pallas_call(
        functools.partial(near_kernel, n),
        grid=(heads,),
        out_shape=(
            f32, f32, f32,
            jax.ShapeDtypeStruct(send.shape, send.dtype),
            jax.ShapeDtypeStruct((2, tokens, width), BF16),
        ),
        in_specs=[col(tokens), col(tokens), col(tokens), col(past), col(past),
                  pl.BlockSpec(bias.shape, lambda h: (0, 0)), hbm, hbm, hbm],
        out_specs=(col(tokens), col(tokens), col(tokens), hbm, hbm),
        scratch_shapes=[dma((n,)), dma((n,)), dma((2,)), dma((2,)), dma],
        compiler_params=pltpu.CompilerParams(
            collective_id=0, has_side_effects=True, vmem_limit_bytes=32 * 2**20
        ),
        name="near",
    )(q, ck, cv, pk, pv, bias, ck, cv, send)


def far_kernel(picks, list_len, place, q, part, got, bias, acc, mx, tot, out):
    tokens = q.shape[0]
    length = tokens // bias.shape[0]
    k_half, v_half = part[0], with_ones(part[1])
    for r in range(0, tokens, ROWS):
        qr = q[r : r + ROWS, :]
        first, count = r // length, ROWS // length
        s_half = scores_of(qr, k_half) + row_bias(bias, first, count, length)
        s_list, v_list = [], []
        for b in range(first, first + count):
            places = [place[b * list_len + j] for j in range(list_len)]
            keys = [got[p // picks, 0, p % picks] for p in places]
            values = [got[p // picks, 1, p % picks] for p in places]
            s_list.append(
                scores_of(q[b * length : (b + 1) * length, :], jnp.concatenate(keys, axis=0))
            )
            v_list.append(with_ones(jnp.concatenate(values, axis=0)))
        s_far = jnp.concatenate(s_list, axis=0)
        m_old = mx[r : r + ROWS, :]
        m_new = jnp.maximum(s_half.max(-1, keepdims=True), s_far.max(-1, keepdims=True)) * FACTOR
        m = jnp.maximum(m_old, jnp.broadcast_to(m_new, m_old.shape))
        keep = jnp.exp2(m_old - m)
        m1 = m[:, :1]
        w_half = jnp.exp2(s_half * FACTOR - m1).astype(BF16)
        w_far = jnp.exp2(s_far * FACTOR - m1).astype(BF16)
        both = jnp.dot(w_half, v_half, preferred_element_type=F32)
        both = both + jnp.concatenate(
            [
                jnp.dot(w_far[i * length : (i + 1) * length], v, preferred_element_type=F32)
                for i, v in enumerate(v_list)
            ],
            axis=0,
        )
        total = tot[r : r + ROWS, :] * keep + both[:, HD:]
        mixed = acc[r : r + ROWS, :] * keep + both[:, :HD]
        out[r : r + ROWS, :] = (mixed / total).astype(out.dtype)


def far(place, q, part, got, bias, acc, mx, tot, list_len):
    tokens, width = q.shape
    n, _, picks, block_len, _ = got.shape

    def col(rows):
        return pl.BlockSpec((rows, HD), lambda h: (0, h))

    return pl.pallas_call(
        functools.partial(far_kernel, picks, list_len),
        grid=(width // HD,),
        out_shape=jax.ShapeDtypeStruct((tokens, width), BF16),
        in_specs=[
            pl.BlockSpec(memory_space=pltpu.SMEM),
            col(tokens),
            pl.BlockSpec((2, tokens, HD), lambda h: (0, 0, h)),
            pl.BlockSpec((n, 2, picks, block_len, HD), lambda h: (0, 0, 0, 0, h)),
            pl.BlockSpec(bias.shape, lambda h: (0, 0)),
            col(tokens), col(tokens), col(tokens),
        ],
        out_specs=col(tokens),
        compiler_params=pltpu.CompilerParams(vmem_limit_bytes=32 * 2**20),
        name="far",
    )(place, q, part, got, bias, acc, mx, tot)


def plan(pattern, read_blocks, past_count, length, n, me):
    blocks, list_len = pattern.shape[0], read_blocks.shape[1]
    entries = blocks * list_len
    picks = entries // n
    parity = me % 2
    own = lax.dynamic_slice_in_dim(pattern, parity * blocks, blocks, 1)
    other = lax.dynamic_slice_in_dim(pattern, (1 - parity) * blocks, blocks, 1)
    own = (own > 0) | (jnp.arange(blocks)[:, None] == jnp.arange(blocks)[None, :])
    bias = [
        jnp.repeat(jnp.where(o, 0.0, NEG).astype(F32), length, axis=1) for o in (own, other > 0)
    ]
    lists = read_blocks.reshape(n, entries)
    earlier = jnp.arange(entries)[None, :] < jnp.arange(entries)[:, None]
    mine = lists // past_count == me
    rank = jnp.sum(jnp.where(earlier[None], mine[:, None, :], False).astype(jnp.int32), axis=2)
    hit = mine[:, None, :] & (rank[:, None, :] == jnp.arange(picks)[None, :, None])
    wanted = jnp.sum(jnp.where(hit, (lists - me * past_count)[:, None, :], 0), axis=2)
    my_list = lax.dynamic_index_in_dim(lists, me, 0, keepdims=False) // past_count
    same = (my_list[None, :] == my_list[:, None]) & earlier
    place = my_list * picks + jnp.sum(same.astype(jnp.int32), axis=1)
    return bias[0], bias[1], wanted.reshape(-1).astype(jnp.int32), place.astype(jnp.int32)


def local(queries, cur_keys, cur_values, past_keys, past_values, pattern, read_blocks, out_weight):
    n = lax.axis_size("loop")
    me = lax.axis_index("loop")
    past_count, block_len, width = past_keys.shape
    length = queries.shape[0] // pattern.shape[0]
    list_len = read_blocks.shape[1]
    weight = lax.all_gather(out_weight, "loop", axis=0, tiled=True)
    bias_own, bias_other, wanted, place = plan(pattern, read_blocks, past_count, length, n, me)
    send = pick_blocks(wanted, past_keys, past_values, n, wanted.shape[0] // n)
    acc, mx, tot, got, part = near(
        queries, cur_keys, cur_values,
        past_keys.reshape(past_count * block_len, width),
        past_values.reshape(past_count * block_len, width),
        bias_own, send, n,
    )
    attended = far(place, queries, part, got, bias_other, acc, mx, tot, list_len)
    return jnp.dot(attended, weight, preferred_element_type=F32).astype(BF16)


def solution(mesh):
    return jax.shard_map(
        local,
        mesh=mesh,
        in_specs=(
            P(("groups", "loop"), None),
            P(("groups", "loop"), None),
            P(("groups", "loop"), None),
            P(("groups", "loop"), None, None),
            P(("groups", "loop"), None, None),
            P(("groups", "loop"), None),
            P("groups", None),
            P("loop", None),
        ),
        out_specs=P(("groups", "loop"), None),
        check_vma=False,
    )
```

time: 444 us -> 365 us (0.82)
  Pallas kernels: 0 us -> 312 us
  matrix products: 120 us -> 20.9 us
  blocking collectives: 93.4 us -> 0 us
  waiting for transfers between devices: 67 us -> 0.71 us
  other arithmetic: 64.1 us -> 1.55 us
  local copies, waits for them, and re-layouts: 72.6 us -> 15.8 us
  starting transfers between devices: 8.67 us -> 0.01 us
    pallas_call x0 -> x3, Pallas kernels: none -> 312 us  [the longest x1 161 us: pick_blocks(): pl.pallas_call(functools.partial(pick_kernel, n, picks), out_shape=jax.Sh...]
    dot_general x31 -> x1, matrix products: 120 us -> 20.9 us  [local(): return jnp.dot(attended, weight, preferred_element_type=F32).astype(BF16)]
    all_to_all x1 -> x0, blocking collectives: 93.4 us -> none  [local(): lax.all_to_all(send_keys, 'loop', split_axis=0, concat_axis=0, tiled=True)]
    all_to_all x1 -> x0, waiting for transfers between devices: 66.3 us -> none  [local(): lax.all_to_all(send_values, 'loop', split_axis=0, concat_axis=0, tiled=True)]
    reduce_sum x15 -> x3, other arithmetic: 42.6 us -> 0.64 us  [the longest x1 0.35 us: plan(): jnp.sum(jnp.where(earlier[None], mine[:, None, :], False).astype(jnp.int3...]
    dynamic_slice x41 -> x0, local copies, waits for them, and re-layouts: 38.5 us -> none  [the longest x40 38.3 us: take_cols(): lax.dynamic_slice_in_dim(values, col_start, group_width, values.ndim - 1)]
    gather x9 -> x0, local copies, waits for them, and re-layouts: 18.5 us -> none  [the longest x1 5.19 us: local(): jnp.take(past_values, wanted.reshape(-1), axis=0)]
    concatenate x2 -> x0, other arithmetic: 10.4 us -> none  [the longest x1 5.61 us: local(): sess_values = jnp.concatenate([cur_values, partner_values], axis=0)]
  transfers between devices with their start and end apart: 4 -> 1, of which waited for: 1 -> 0; matrix products, arithmetic and copies ran while one was open for 54% -> 1% of each run, Pallas kernels for 0% -> 86%
where the time goes in v1:
time: 365 us
  Pallas kernels  312 us (85%)
  matrix products  20.9 us (6%)
  local copies, waits for them, and re-layouts  15.8 us (4%)
  between operations  13.5 us (4%)
    pallas_call x1, Pallas kernels, pick_blocks(): pl.pallas_call(functools.partial(pick_kernel, n, picks), out_shape=jax.Sh...  161 us
    pallas_call x1, Pallas kernels, near(): pl.pallas_call(functools.partial(near_kernel, n), grid=(heads,), out_shap...  120 us
    pallas_call x1, Pallas kernels, far(): pl.pallas_call(functools.partial(far_kernel, picks, list_len), grid=(widt...  31.3 us
    dot_general x1, matrix products, local(): return jnp.dot(attended, weight, preferred_element_type=F32).astype(BF16)  20.9 us
    unnamed x20, local copies, waits for them, and re-layouts  15 us
  transfers between devices with their start and end apart: 1, of which 0 were waited for; matrix products, arithmetic and copies ran while one was open for 1% of the time, Pallas kernels for 86%

profile of v1, /device:TPU:13, one launch (start us, length us, event | category | flops | bytes accessed | tf_op | source)
XLA Modules:
  0.0 364.6 jit_solution(14692461560302993785)
XLA Ops:
  6.5 0.0 all-gather.2.cloned.1.call-start
  6.5 0.7 all-gather.2.cloned.1.call-update
  7.3 0.8 fusion.5
  8.1 0.1 broadcast_bitcast_fusion
  8.2 0.8 copy.10
  9.0 0.1 reshape.83
  9.1 0.3 convert_reduce_fusion
  9.4 0.1 select_reduce_fusion
  9.6 0.1 copy.11
  9.6 0.6 reshape.87.wanted
  10.3 0.0 copy-start.2
  10.3 161.3 %pick.1.send = bf16[16,2,2,16,2560]{4,3,2,1,0:T(8,128)(2,1)} custom-call(s32[32]{0:T(128)} %reshape.87.wanted, bf16[48,16,2560]{2,1,0:T(8,128)(2,1)} %pk.1, bf16[48,16,2560]{2,1,0:T(8,128)(2,1)} %pv.1), custom_call_target="tpu_custom_call" | custom-call | tf_op jit(solution)/shard_map/pick/pallas_call | solution.py:57
  171.6 0.0 copy-done.2
  171.6 0.0 copy-start
  171.6 2.1 copy-done
  173.7 0.0 copy-start.1
  173.7 2.1 copy-done.1
  175.8 0.0 copy-start.3
  175.8 1.7 copy-done.3
  177.5 0.0 copy-start.4
  177.5 1.7 copy-done.4
  179.3 119.6 %near.1 = (f32[512,2560]{1,0:T(8,128)S(1)}, f32[512,2560]{1,0:T(8,128)}, f32[512,2560]{1,0:T(8,128)}, bf16[16,2,2,16,2560]{4,3,2,1,0:T(8,128)(2,1)}, bf16[2,512,2560]{2,1,0:T(8,128)(2,1)}) custom-call(bf16[512,2560]{1,0:T(8,128)(2,1)S(1)} %copy-done.2, bf16[512,2560]{1,0:T(8,128)(2,1)S(1)} %copy-done.3, bf16[512,2560]{1,0:T(8,128)(2,1)S(1)} %copy-done.4, ...), custom_call_target="tpu_custom_call" | custom-call | tf_op jit(solution)/shard_map/near/pallas_call | solution.py:158
  299.0 0.2 convert_reduce_fusion.1
  299.1 0.0 copy-start.5
  299.2 2.5 copy-done.5
  301.6 0.0 copy-start.6
  301.6 2.5 copy-done.6
  304.1 31.3 %far.1 = bf16[512,2560]{1,0:T(8,128)(2,1)S(1)} custom-call(s32[32]{0:T(128)S(1)} %multiply_add_fusion.place, bf16[512,2560]{1,0:T(8,128)(2,1)S(1)} %copy-done.2, bf16[2,512,2560]{2,1,0:T(8,128)(2,1)S(1)} %copy-done.6, bf16[16,2,2,16,2560]{4,3,2,1,0:T(8,128)(2,1)S(1)} %copy-done.5, f32[4,512]{1,0:T(4,128)S(1)} %bitcast.23, ...), custom_call_target="tpu_custom_call" | custom-call | tf_op jit(solution)/shard_map/far/pallas_call | solution.py:222
  335.4 0.0 copy-start.7
  335.4 1.5 copy-done.7
  336.9 0.0 all-gather.2.cloned.1.call-done
  336.9 20.9 %convolution_convert_fusion = bf16[512,5120]{1,0:T(8,128)(2,1)} fusion(bf16[512,2560]{1,0:T(8,128)(2,1)} %copy-done.7, bf16[2560,5120]{1,0:T(8,128)(2,1)} %all-gather.2.cloned.1.call-done), kind=kOutput, calls=%fused_computation | convolution fusion | flops 13424394240 | bytes 34078720 | tf_op jit(solution)/shard_map/dot_general | solution.py:279
  (8 shorter events, 0.1 us)
Async XLA Ops:
  6.5 330.3 %all-gather.2.cloned.1.call-start = ((), (), s32[]{:S(2)}) async-start(), calls=%async_computation | async-start | bytes 27852800 | tf_op jit(solution)/shard_map/all_gather | solution.py:269
  10.3 161.3 %copy-start.2 = (bf16[512,2560]{1,0:T(8,128)(2,1)S(1)}, bf16[512,2560]{1,0:T(8,128)(2,1)}, u32[]{:S(2)}) copy-start(bf16[512,2560]{1,0:T(8,128)(2,1)} %q.3) | copy-start | bytes 7864324
  171.6 2.1 copy-start
  173.7 2.1 copy-start.1
  175.8 1.7 copy-start.3
  177.5 1.7 copy-start.4
  299.1 2.5 copy-start.5
  301.6 2.5 copy-start.6
  335.4 1.5 copy-start.7
Sparse Core Ops, SparseCore 0:
  9.0 212.0 all-gather.1

commit v2 on v1

--- a/solution.py
+++ b/solution.py
@@ -12,6 +12,7 @@
 NEG = -1e30
 ROWS = 256
 FACTOR = HD**-0.5 * math.log2(math.e)
+ROOM = 60 * 2**20
 MESH = pl.DeviceIdType.MESH
 F32 = jnp.float32
 BF16 = jnp.bfloat16
@@ -33,37 +34,24 @@
     return jnp.concatenate(rows, axis=0)
 
 
-def pick_kernel(n, picks, wanted, pk, pv, send, sem):
-    def copies(i):
-        reader, pick = i // picks, i % picks
-        block = wanted[i]
-        return (
-            pltpu.make_async_copy(pk.at[block], send.at[reader, 0, pick], sem.at[2 * i]),
-            pltpu.make_async_copy(pv.at[block], send.at[reader, 1, pick], sem.at[2 * i + 1]),
-        )
-
-    @pl.loop(0, n * picks)
-    def _(i):
-        for c in copies(i):
-            c.start()
-
-    @pl.loop(0, n * picks)
-    def _(i):
-        for c in copies(i):
-            c.wait()
+def pick_kernel(wanted, pk, pv, send):
+    send[0, 0, 0] = pk[0]
+    send[0, 1, 0] = pv[0]
 
 
 def pick_blocks(wanted, pk, pv, n, picks):
+    block = pl.BlockSpec((1,) + pk.shape[1:], lambda r, p, wanted: (wanted[r * picks + p], 0, 0))
     return pl.pallas_call(
-        functools.partial(pick_kernel, n, picks),
+        pick_kernel,
         out_shape=jax.ShapeDtypeStruct((n, 2, picks) + pk.shape[1:], pk.dtype),
-        in_specs=[
-            pl.BlockSpec(memory_space=pltpu.SMEM),
-            pl.BlockSpec(memory_space=pl.ANY),
-            pl.BlockSpec(memory_space=pl.ANY),
-        ],
-        out_specs=pl.BlockSpec(memory_space=pl.ANY),
-        scratch_shapes=[pltpu.SemaphoreType.DMA((2 * n * picks,))],
+        grid_spec=pltpu.PrefetchScalarGridSpec(
+            num_scalar_prefetch=1,
+            grid=(n, picks),
+            in_specs=[block, block],
+            out_specs=pl.BlockSpec(
+                (1, 2, 1) + pk.shape[1:], lambda r, p, wanted: (r, 0, p, 0, 0)
+            ),
+        ),
         name="pick",
     )(wanted, pk, pv)
 
@@ -168,7 +156,12 @@
         out_specs=(col(tokens), col(tokens), col(tokens), hbm, hbm),
         scratch_shapes=[dma((n,)), dma((n,)), dma((2,)), dma((2,)), dma],
         compiler_params=pltpu.CompilerParams(
-            collective_id=0, has_side_effects=True, vmem_limit_bytes=32 * 2**20
+            collective_id=0, has_side_effects=True, vmem_limit_bytes=ROOM
+        ),
+        cost_estimate=pl.CostEstimate(
+            flops=60 * tokens * (tokens + past) * width,
+            bytes_accessed=40 * tokens * width,
+            transcendentals=tokens * (tokens + past) * heads,
         ),
         name="near",
     )(q, ck, cv, pk, pv, bias, ck, cv, send)
@@ -232,7 +225,12 @@
             col(tokens), col(tokens), col(tokens),
         ],
         out_specs=col(tokens),
-        compiler_params=pltpu.CompilerParams(vmem_limit_bytes=32 * 2**20),
+        compiler_params=pltpu.CompilerParams(vmem_limit_bytes=ROOM),
+        cost_estimate=pl.CostEstimate(
+            flops=12 * tokens * tokens * width,
+            bytes_accessed=30 * tokens * width,
+            transcendentals=2 * tokens * tokens * (width // HD),
+        ),
         name="far",
     )(place, q, part, got, bias, acc, mx, tot)
 
@@ -260,13 +258,64 @@
     return bias[0], bias[1], wanted.reshape(-1).astype(jnp.int32), place.astype(jnp.int32)
 
 
+def project_kernel(side, attended, weight, *rest):
+    rest[-1][...] = jnp.dot(
+        attended[...], weight[...], preferred_element_type=F32
+    ).astype(BF16)
+
+
+def project(side, attended, weight, done, tile):
+    tokens, width = attended.shape
+    columns = weight.shape[1]
+    tiles = columns // tile
+    more = [] if done is None else [done]
+    return pl.pallas_call(
+        project_kernel,
+        out_shape=jax.ShapeDtypeStruct((tokens, 2 * columns), BF16),
+        grid_spec=pltpu.PrefetchScalarGridSpec(
+            num_scalar_prefetch=1,
+            grid=(tiles,),
+            in_specs=[
+                pl.BlockSpec((tokens, width), lambda t, side: (0, 0)),
+                pl.BlockSpec((width, tile), lambda t, side: (0, t)),
+            ]
+            + [pl.BlockSpec(memory_space=pl.ANY)] * len(more),
+            out_specs=pl.BlockSpec((tokens, tile), lambda t, side: (0, side[0] * tiles + t)),
+        ),
+        input_output_aliases={} if done is None else {3: 0},
+        compiler_params=pltpu.CompilerParams(vmem_limit_bytes=ROOM),
+        cost_estimate=pl.CostEstimate(
+            flops=2 * tokens * width * columns,
+            bytes_accessed=2 * (width * columns + tokens * (width + columns)),
+            transcendentals=0,
+        ),
+        name="project",
+    )(side, attended, weight, *more)
+
+
+def swap_cores(value, n):
+    return lax.ppermute(value, "loop", [(i, i ^ 1) for i in range(n)])
+
+
+def gather_half(out_weight, n, me):
+    half = out_weight.shape[1] // 2
+    parity = me % 2
+    mine = lax.dynamic_slice_in_dim(out_weight, parity * half, half, 1)
+    its = swap_cores(lax.dynamic_slice_in_dim(out_weight, (1 - parity) * half, half, 1), n)
+    rows = jnp.concatenate(
+        [jnp.where(parity == 0, mine, its), jnp.where(parity == 0, its, mine)], axis=0
+    )
+    groups = [list(range(c, n, 2)) for c in range(2)]
+    return lax.all_gather(rows, "loop", axis=0, tiled=True, axis_index_groups=groups)
+
+
 def local(queries, cur_keys, cur_values, past_keys, past_values, pattern, read_blocks, out_weight):
     n = lax.axis_size("loop")
     me = lax.axis_index("loop")
     past_count, block_len, width = past_keys.shape
     length = queries.shape[0] // pattern.shape[0]
     list_len = read_blocks.shape[1]
-    weight = lax.all_gather(out_weight, "loop", axis=0, tiled=True)
+    my_half = gather_half(out_weight, n, me)
     bias_own, bias_other, wanted, place = plan(pattern, read_blocks, past_count, length, n, me)
     send = pick_blocks(wanted, past_keys, past_values, n, wanted.shape[0] // n)
     acc, mx, tot, got, part = near(
@@ -275,8 +324,12 @@
         past_values.reshape(past_count * block_len, width),
         bias_own, send, n,
     )
+    my_half, got = lax.optimization_barrier((my_half, got))
     attended = far(place, queries, part, got, bias_other, acc, mx, tot, list_len)
-    return jnp.dot(attended, weight, preferred_element_type=F32).astype(BF16)
+    its_half = swap_cores(my_half, n)
+    side = (me % 2).astype(jnp.int32).reshape(1)
+    done = project(side, attended, my_half, None, 512)
+    return project(1 - side, attended, its_half, done, 512)
 
 
 def solution(mesh):

time: 365 us -> 365 us (level); the launches traced: 365 us -> 358 us
  waiting for transfers between devices: 0.71 us -> 31 us
  matrix products: 20.9 us -> 0 us
  local copies, waits for them, and re-layouts: 15.8 us -> 3.44 us
  Pallas kernels: 312 us -> 305 us
    pallas_call x1 -> x3, Pallas kernels: 161 us -> 42.8 us  [the longest x2 23.6 us: project(): pl.pallas_call(project_kernel, out_shape=jax.ShapeDtypeStruct((tokens, 2...]
    pallas_call x1, Pallas kernels: 120 us -> 232 us  [near(): pl.pallas_call(functools.partial(near_kernel, n), grid=(heads,), out_shap...]
    all_gather x1, waiting for transfers between devices: 0.01 us -> 29 us  [gather_half(): lax.all_gather(rows, 'loop', axis=0, tiled=True, axis_index_groups=groups)]
    dot_general x1 -> x0, matrix products: 20.9 us -> none  [local(): return jnp.dot(attended, weight, preferred_element_type=F32).astype(BF16)]
    unnamed x20 -> x9, local copies, waits for them, and re-layouts: 15 us -> 1.45 us
  transfers between devices with their start and end apart: 1 -> 3, of which waited for: 0 -> 2; matrix products, arithmetic and copies ran while one was open for 1% -> 1% of each run, Pallas kernels for 86% -> 82%
where the time goes in v2:
time: 365 us; the launch traced here: 358 us
  Pallas kernels  305 us (84%)
  waiting for transfers between devices  31 us (8%)
  between operations  13.5 us (4%)
  other arithmetic  4 us (1%)
    pallas_call x1, Pallas kernels, near(): pl.pallas_call(functools.partial(near_kernel, n), grid=(heads,), out_shap...  232 us
    pallas_call x1, Pallas kernels, far(): pl.pallas_call(functools.partial(far_kernel, picks, list_len), grid=(widt...  29.5 us
    all_gather x1, waiting for transfers between devices, gather_half(): lax.all_gather(rows, 'loop', axis=0, tiled=True, axis_index_groups=groups)  29 us
    pallas_call x2, Pallas kernels, project(): pl.pallas_call(project_kernel, out_shape=jax.ShapeDtypeStruct((tokens, 2...  23.6 us
    pallas_call x1, Pallas kernels, pick_blocks(): pl.pallas_call(pick_kernel, out_shape=jax.ShapeDtypeStruct((n, 2, picks)...  19.2 us
  transfers between devices with their start and end apart: 3, of which 2 were waited for; matrix products, arithmetic and copies ran while one was open for 1% of the time, Pallas kernels for 82%

profile of v2, /device:TPU:13, one launch (start us, length us, event | category | flops | bytes accessed | tf_op | source)
XLA Modules:
  0.0 357.6 jit_solution(12877924255413316976)
XLA Ops:
  6.5 0.0 all-gather.2.cloned.1.call-start
  6.5 1.2 constant_dynamic-slice_fusion
  7.7 0.7 collective-permute-start
  8.5 2.0 collective-permute-done
  10.4 1.4 broadcast_select_fusion.1
  11.9 0.0 copy-start
  11.9 0.0 copy-start.1
  11.9 1.3 pad_maximum_fusion
  13.1 0.0 all-gather.2.cloned.1.call-update
  13.2 0.0 copy-done
  13.2 0.1 fusion.5
  13.3 0.1 broadcast_bitcast_fusion.1
  13.3 0.6 copy.18
  13.9 0.0 copy-done.1
  14.0 0.1 copy.11
  14.0 0.1 reshape.87
  14.1 0.3 convert_reduce_fusion
  14.5 0.1 select_reduce_fusion
  14.6 0.1 copy.12
  14.7 0.6 reshape.91.wanted
  15.3 19.2 %pick.1.send = bf16[16,2,2,16,2560]{4,3,2,1,0:T(8,128)(2,1)} custom-call(s32[32]{0:T(128)} %reshape.91.wanted, bf16[48,16,2560]{2,1,0:T(8,128)(2,1)} %pk.1, bf16[48,16,2560]{2,1,0:T(8,128)(2,1)} %pv.1), custom_call_target="tpu_custom_call" | custom-call | tf_op jit(solution)/shard_map/pick/pallas_call | solution.py:44
  34.5 232.3 %near.1 = (f32[512,2560]{1,0:T(8,128)}, f32[512,2560]{1,0:T(8,128)}, f32[512,2560]{1,0:T(8,128)}, bf16[16,2,2,16,2560]{4,3,2,1,0:T(8,128)(2,1)}, bf16[2,512,2560]{2,1,0:T(8,128)(2,1)}) custom-call(bf16[512,2560]{1,0:T(8,128)(2,1)} %q.3, bf16[512,2560]{1,0:T(8,128)(2,1)} %ck_all.1, bf16[512,2560]{1,0:T(8,128)(2,1)} %cv_all.1, bf16[768,2560]{1,0:T(8,128)(2,1)} %bitcast.19, ...), custom_call_target="tpu_custom_call" | custom-call | flops 100663296000 | bytes 52428800 | tf_op jit(solution)/shard_map/near/pallas_call | solution.py:146
  266.8 29.0 %all-gather.2.cloned.1.call-done.weight = bf16[2560,2560]{1,0:T(8,128)(2,1)} async-done(((bf16[320,2560]{1,0:T(8,128)(2,1)}), bf16[2560,2560]{1,0:T(8,128)(2,1)}) %all-gather.2.cloned.1.call-update) | async-done | bytes 13107216 | tf_op jit(solution)/shard_map/all_gather | solution.py:309
  295.8 0.4 collective-permute-start.1
  296.3 0.1 broadcast_bitcast_fusion
  296.3 0.6 copy.17
  297.0 0.2 convert_reduce_fusion.1
  297.1 0.5 multiply_add_fusion.place
  297.7 29.5 %far.1.attended = bf16[512,2560]{1,0:T(8,128)(2,1)} custom-call(s32[32]{0:T(128)} %multiply_add_fusion.place, bf16[512,2560]{1,0:T(8,128)(2,1)} %q.3, bf16[2,512,2560]{2,1,0:T(8,128)(2,1)} %get-tuple-element.12.part, bf16[16,2,2,16,2560]{4,3,2,1,0:T(8,128)(2,1)} %get-tuple-element.14.got, f32[4,512]{1,0:T(4,128)} %bitcast.21, ...), custom_call_target="tpu_custom_call" | custom-call | flops 8053063680 | bytes 39321600 | tf_op jit(solution)/shard_map/far/pallas_call | solution.py:215
  327.2 11.8 %project.2.rest_0_ = bf16[512,5120]{1,0:T(8,128)(2,1)} custom-call(s32[1]{0:T(128)} %bitcast.side, bf16[512,2560]{1,0:T(8,128)(2,1)} %far.1.attended, bf16[2560,2560]{1,0:T(8,128)(2,1)} %all-gather.2.cloned.1.call-done.weight), custom_call_target="tpu_custom_call" | custom-call | flops 6710886400 | bytes 18350080 | tf_op jit(solution)/shard_map/project/pallas_call | solution.py:272
  339.0 0.0 collective-permute-done.1.weight
  339.0 11.8 %project.3 = bf16[512,5120]{1,0:T(8,128)(2,1)} custom-call(s32[1]{0:T(128)S(6)} %sub.31.side, bf16[512,2560]{1,0:T(8,128)(2,1)} %far.1.attended, bf16[2560,2560]{1,0:T(8,128)(2,1)} %collective-permute-done.1.weight, bf16[512,5120]{1,0:T(8,128)(2,1)} %project.2.rest_0_), custom_call_target="tpu_custom_call", output_to_operand_aliasing={{}: (3, {})} | custom-call | flops 6710886400 | bytes 18350080 | tf_op jit(solution)/shard_map/project/pallas_call | solution.py:272
  (5 shorter events, 0.1 us)
Async XLA Ops:
  6.5 289.3 %all-gather.2.cloned.1.call-start = ((), (), s32[]{:S(2)}) async-start(), calls=%async_computation | async-start | bytes 14745600 | tf_op jit(solution)/shard_map/all_gather | solution.py:309
  7.7 2.7 collective-permute-start
  11.9 1.3 copy-start
  11.9 2.1 copy-start.1
  295.8 43.2 %collective-permute-start.1 = (bf16[2560,2560]{1,0:T(8,128)(2,1)}, bf16[2560,2560]{1,0:T(8,128)(2,1)}, u32[]{:S(2)}, u32[]{:S(2)}) collective-permute-start(bf16[2560,2560]{1,0:T(8,128)(2,1)} %all-gather.2.cloned.1.call-done.weight), channel_id=1, source_target_pairs={{0,1},{1,0},{2,3},{3,2},{4,5},{5,4},{6,7},{7,6},{8,9},{9,8},{10,11... | collective-permute-start | bytes 39321608 | tf_op jit(solution)/shard_map/ppermute | solution.py:297
Sparse Core Ops, SparseCore 0:
  13.3 282.4 all-gather.1

commit v3 on v2

--- a/solution.py
+++ b/solution.py
@@ -258,29 +258,28 @@
     return bias[0], bias[1], wanted.reshape(-1).astype(jnp.int32), place.astype(jnp.int32)
 
 
-def project_kernel(side, attended, weight, *rest):
+def project_kernel(first, attended, weight, *rest):
     rest[-1][...] = jnp.dot(
         attended[...], weight[...], preferred_element_type=F32
     ).astype(BF16)
 
 
-def project(side, attended, weight, done, tile):
+def project(first, attended, weight, done, whole, tile):
     tokens, width = attended.shape
     columns = weight.shape[1]
-    tiles = columns // tile
     more = [] if done is None else [done]
     return pl.pallas_call(
         project_kernel,
-        out_shape=jax.ShapeDtypeStruct((tokens, 2 * columns), BF16),
+        out_shape=jax.ShapeDtypeStruct((tokens, whole), BF16),
         grid_spec=pltpu.PrefetchScalarGridSpec(
             num_scalar_prefetch=1,
-            grid=(tiles,),
+            grid=(columns // tile,),
             in_specs=[
-                pl.BlockSpec((tokens, width), lambda t, side: (0, 0)),
-                pl.BlockSpec((width, tile), lambda t, side: (0, t)),
+                pl.BlockSpec((tokens, width), lambda t, first: (0, 0)),
+                pl.BlockSpec((width, tile), lambda t, first: (0, t)),
             ]
             + [pl.BlockSpec(memory_space=pl.ANY)] * len(more),
-            out_specs=pl.BlockSpec((tokens, tile), lambda t, side: (0, side[0] * tiles + t)),
+            out_specs=pl.BlockSpec((tokens, tile), lambda t, first: (0, first[0] + t)),
         ),
         input_output_aliases={} if done is None else {3: 0},
         compiler_params=pltpu.CompilerParams(vmem_limit_bytes=ROOM),
@@ -290,46 +289,38 @@
             transcendentals=0,
         ),
         name="project",
-    )(side, attended, weight, *more)
-
-
-def swap_cores(value, n):
-    return lax.ppermute(value, "loop", [(i, i ^ 1) for i in range(n)])
-
-
-def gather_half(out_weight, n, me):
-    half = out_weight.shape[1] // 2
-    parity = me % 2
-    mine = lax.dynamic_slice_in_dim(out_weight, parity * half, half, 1)
-    its = swap_cores(lax.dynamic_slice_in_dim(out_weight, (1 - parity) * half, half, 1), n)
-    rows = jnp.concatenate(
-        [jnp.where(parity == 0, mine, its), jnp.where(parity == 0, its, mine)], axis=0
-    )
-    groups = [list(range(c, n, 2)) for c in range(2)]
-    return lax.all_gather(rows, "loop", axis=0, tiled=True, axis_index_groups=groups)
+    )(first.astype(jnp.int32).reshape(1), attended, weight, *more)
 
 
 def local(queries, cur_keys, cur_values, past_keys, past_values, pattern, read_blocks, out_weight):
     n = lax.axis_size("loop")
+    groups = lax.axis_size("groups")
     me = lax.axis_index("loop")
+    side = lax.axis_index("groups") % 2
     past_count, block_len, width = past_keys.shape
     length = queries.shape[0] // pattern.shape[0]
     list_len = read_blocks.shape[1]
-    my_half = gather_half(out_weight, n, me)
+    whole = out_weight.shape[1]
+    piece = whole // 5
+    tile = piece // 2
+    mine = lax.all_gather(
+        lax.dynamic_slice_in_dim(out_weight, side * piece, piece, 1), "loop", axis=0, tiled=True
+    )
+    rest = lax.all_gather(out_weight[:, 2 * piece :], "loop", axis=0, tiled=True)
     bias_own, bias_other, wanted, place = plan(pattern, read_blocks, past_count, length, n, me)
     send = pick_blocks(wanted, past_keys, past_values, n, wanted.shape[0] // n)
+    mine, send = lax.optimization_barrier((mine, send))
+    its = lax.ppermute(mine, "groups", [(i, i ^ 1) for i in range(groups)])
     acc, mx, tot, got, part = near(
         queries, cur_keys, cur_values,
         past_keys.reshape(past_count * block_len, width),
         past_values.reshape(past_count * block_len, width),
         bias_own, send, n,
     )
-    my_half, got = lax.optimization_barrier((my_half, got))
     attended = far(place, queries, part, got, bias_other, acc, mx, tot, list_len)
-    its_half = swap_cores(my_half, n)
-    side = (me % 2).astype(jnp.int32).reshape(1)
-    done = project(side, attended, my_half, None, 512)
-    return project(1 - side, attended, its_half, done, 512)
+    done = project(2 * side, attended, mine, None, whole, tile)
+    done = project(2 - 2 * side, attended, its, done, whole, tile)
+    return project(jnp.full((), 4), attended, rest, done, whole, tile)
 
 
 def solution(mesh):

time: 365 us -> 347 us (0.951); the launches traced: 358 us -> 344 us
  Pallas kernels: 305 us -> 289 us
    pallas_call x1, Pallas kernels: 232 us -> 214 us  [near(): pl.pallas_call(functools.partial(near_kernel, n), grid=(heads,), out_shap...]
    pallas_call x2 -> x3, Pallas kernels: 23.6 us -> 26.3 us  [project(): pl.pallas_call(project_kernel, out_shape=jax.ShapeDtypeStruct((tokens, wh...]
    all_gather x1 -> x2, waiting for transfers between devices: 29 us -> 31.6 us  [the longest x1 31.6 us: local(): lax.all_gather(lax.dynamic_slice_in_dim(out_weight, side * piece, piece,...]
  transfers between devices with their start and end apart: 3 -> 3, of which waited for: 2 -> 1; matrix products, arithmetic and copies ran while one was open for 1% -> 2% of each run, Pallas kernels for 82% -> 80%
where the time goes in v3:
time: 347 us; the launch traced here: 344 us
  Pallas kernels  289 us (83%)
  waiting for transfers between devices  31.7 us (9%)
  between operations  13.5 us (4%)
  local copies, waits for them, and re-layouts  6.86 us (2%)
    pallas_call x1, Pallas kernels, near(): pl.pallas_call(functools.partial(near_kernel, n), grid=(heads,), out_shap...  214 us
    all_gather x1, waiting for transfers between devices, local(): lax.all_gather(lax.dynamic_slice_in_dim(out_weight, side * piece, piece,...  31.6 us
    pallas_call x1, Pallas kernels, far(): pl.pallas_call(functools.partial(far_kernel, picks, list_len), grid=(widt...  29.5 us
    pallas_call x3, Pallas kernels, project(): pl.pallas_call(project_kernel, out_shape=jax.ShapeDtypeStruct((tokens, wh...  26.3 us
    pallas_call x1, Pallas kernels, pick_blocks(): pl.pallas_call(pick_kernel, out_shape=jax.ShapeDtypeStruct((n, 2, picks)...  19.1 us
  transfers between devices with their start and end apart: 3, of which 1 were waited for; matrix products, arithmetic and copies ran while one was open for 2% of the time, Pallas kernels for 80%

profile of v3, /device:TPU:13, one launch (start us, length us, event | category | flops | bytes accessed | tf_op | source)
XLA Modules:
  0.0 344.2 jit_solution(13328953383088176929)
XLA Ops:
  6.5 0.0 all-gather.3.cloned.1.call-start
  6.5 1.7 constant_dynamic-slice_fusion
  8.3 0.0 all-gather.3.cloned.1.call-update
  8.3 0.0 all-gather.5.cloned.1.call-start
  8.3 2.2 slice.3
  10.6 0.0 all-gather.5.cloned.1.call-update
  10.6 0.8 copy.12
  11.4 0.1 reshape.89
  11.5 0.8 fusion.5
  12.3 0.1 broadcast_bitcast_fusion.1
  12.4 0.6 copy.19
  13.0 0.4 convert_reduce_fusion
  13.4 0.1 select_reduce_fusion
  13.5 0.1 copy.13
  13.6 0.6 reshape.93.wanted
  14.2 0.1 broadcast_bitcast_fusion
  14.3 0.6 copy.18
  14.9 19.1 %pick.1.send = bf16[16,2,2,16,2560]{4,3,2,1,0:T(8,128)(2,1)} custom-call(s32[32]{0:T(128)} %reshape.93.wanted, bf16[48,16,2560]{2,1,0:T(8,128)(2,1)} %pk.1, bf16[48,16,2560]{2,1,0:T(8,128)(2,1)} %pv.1), custom_call_target="tpu_custom_call" | custom-call | tf_op jit(solution)/shard_map/pick/pallas_call | solution.py:44
  33.9 0.2 convert_reduce_fusion.1
  34.1 0.5 multiply_add_fusion.place
  34.7 31.6 %all-gather.3.cloned.1.call-done.weight = bf16[2560,1024]{1,0:T(8,128)(2,1)} async-done(((bf16[160,1024]{1,0:T(8,128)(2,1)}), bf16[2560,1024]{1,0:T(8,128)(2,1)}) %all-gather.3.cloned.1.call-update) | async-done | bytes 5242896 | tf_op jit(solution)/shard_map/all_gather | solution.py:306
  66.3 1.2 collective-permute-start
  67.5 214.0 %near.1 = (f32[512,2560]{1,0:T(8,128)}, f32[512,2560]{1,0:T(8,128)}, f32[512,2560]{1,0:T(8,128)}, bf16[16,2,2,16,2560]{4,3,2,1,0:T(8,128)(2,1)}, bf16[2,512,2560]{2,1,0:T(8,128)(2,1)}) custom-call(bf16[512,2560]{1,0:T(8,128)(2,1)} %q.3, bf16[512,2560]{1,0:T(8,128)(2,1)} %ck_all.1, bf16[512,2560]{1,0:T(8,128)(2,1)} %cv_all.1, bf16[768,2560]{1,0:T(8,128)(2,1)} %bitcast.20, ...), custom_call_target="tpu_custom_call" | custom-call | flops 100663296000 | bytes 52428800 | tf_op jit(solution)/shard_map/near/pallas_call | solution.py:146
  281.5 29.5 %far.1.attended = bf16[512,2560]{1,0:T(8,128)(2,1)} custom-call(s32[32]{0:T(128)} %multiply_add_fusion.place, bf16[512,2560]{1,0:T(8,128)(2,1)} %q.3, bf16[2,512,2560]{2,1,0:T(8,128)(2,1)} %get-tuple-element.13.part, bf16[16,2,2,16,2560]{4,3,2,1,0:T(8,128)(2,1)} %get-tuple-element.14.got, f32[4,512]{1,0:T(4,128)} %bitcast.22, ...), custom_call_target="tpu_custom_call" | custom-call | flops 8053063680 | bytes 39321600 | tf_op jit(solution)/shard_map/far/pallas_call | solution.py:215
  311.1 6.4 %project.3.rest_0_ = bf16[512,5120]{1,0:T(8,128)(2,1)} custom-call(s32[1]{0:T(128)} %bitcast.6.first, bf16[512,2560]{1,0:T(8,128)(2,1)} %far.1.attended, bf16[2560,1024]{1,0:T(8,128)(2,1)} %all-gather.3.cloned.1.call-done.weight), custom_call_target="tpu_custom_call" | custom-call | flops 2684354560 | bytes 8912896 | tf_op jit(solution)/shard_map/project/pallas_call | solution.py:271
  317.5 0.0 collective-permute-done.weight
  317.5 6.4 %project.4.rest_0_ = bf16[512,5120]{1,0:T(8,128)(2,1)} custom-call(s32[1]{0:T(128)} %bitcast.5.first, bf16[512,2560]{1,0:T(8,128)(2,1)} %far.1.attended, bf16[2560,1024]{1,0:T(8,128)(2,1)} %collective-permute-done.weight, bf16[512,5120]{1,0:T(8,128)(2,1)} %project.3.rest_0_), custom_call_target="tpu_custom_call", output_to_operand_aliasing={{}: (3, {})} | custom-call | flops 2684354560 | bytes 8912896 | tf_op jit(solution)/shard_map/project/pallas_call | solution.py:271
  323.9 0.0 all-gather.5.cloned.1.call-done.weight
  323.9 13.5 %project.5 = bf16[512,5120]{1,0:T(8,128)(2,1)} custom-call(s32[1]{0:T(128)} %constant.29.clone.1.first, bf16[512,2560]{1,0:T(8,128)(2,1)} %far.1.attended, bf16[2560,3072]{1,0:T(8,128)(2,1)} %all-gather.5.cloned.1.call-done.weight, bf16[512,5120]{1,0:T(8,128)(2,1)} %project.4.rest_0_), custom_call_target="tpu_custom_call", output_to_operand_aliasing={{}: (3, {})} | custom-call | flops 8053063680 | bytes 21495808 | tf_op jit(solution)/shard_map/project/pallas_call | solution.py:271
  (5 shorter events, 0.1 us)
Async XLA Ops:
  6.5 59.8 %all-gather.3.cloned.1.call-start = ((), (), s32[]{:S(2)}) async-start(), calls=%async_computation | async-start | bytes 5570560 | tf_op jit(solution)/shard_map/all_gather | solution.py:306
  8.3 315.6 %all-gather.5.cloned.1.call-start = ((), (), s32[]{:S(2)}) async-start(), calls=%async_computation.1 | async-start | bytes 16711680 | tf_op jit(solution)/shard_map/all_gather | solution.py:309
  66.3 251.2 %collective-permute-start = (bf16[2560,1024]{1,0:T(8,128)(2,1)}, bf16[2560,1024]{1,0:T(8,128)(2,1)}, u32[]{:S(2)}, u32[]{:S(2)}) collective-permute-start(bf16[2560,1024]{1,0:T(8,128)(2,1)} %all-gather.3.cloned.1.call-done.weight), channel_id=1, source_target_pairs={{0,16},{16,0},{1,17},{17,1},{2,18},{18,2},{3,19},{19,3},{4,20},{20... | collective-permute-start | bytes 15728648 | tf_op jit(solution)/shard_map/ppermute | solution.py:313
Sparse Core Ops, SparseCore 0:
  9.6 56.6 all-gather.2
  68.6 210.5 all-gather.4

commit v4 on v3

--- a/solution.py
+++ b/solution.py
@@ -306,17 +306,18 @@
     mine = lax.all_gather(
         lax.dynamic_slice_in_dim(out_weight, side * piece, piece, 1), "loop", axis=0, tiled=True
     )
-    rest = lax.all_gather(out_weight[:, 2 * piece :], "loop", axis=0, tiled=True)
+    rest = out_weight[:, 2 * piece :]
     bias_own, bias_other, wanted, place = plan(pattern, read_blocks, past_count, length, n, me)
     send = pick_blocks(wanted, past_keys, past_values, n, wanted.shape[0] // n)
-    mine, send = lax.optimization_barrier((mine, send))
-    its = lax.ppermute(mine, "groups", [(i, i ^ 1) for i in range(groups)])
     acc, mx, tot, got, part = near(
         queries, cur_keys, cur_values,
         past_keys.reshape(past_count * block_len, width),
         past_values.reshape(past_count * block_len, width),
         bias_own, send, n,
     )
+    mine, rest, got = lax.optimization_barrier((mine, rest, got))
+    rest = lax.all_gather(rest, "loop", axis=0, tiled=True)
+    its = lax.ppermute(mine, "groups", [(i, i ^ 1) for i in range(groups)])
     attended = far(place, queries, part, got, bias_other, acc, mx, tot, list_len)
     done = project(2 * side, attended, mine, None, whole, tile)
     done = project(2 - 2 * side, attended, its, done, whole, tile)

time: 347 us -> 320 us (0.922)
  Pallas kernels: 289 us -> 217 us
  waiting for transfers between devices: 31.7 us -> 75.8 us
    ppermute x1, waiting for transfers between devices: 0.01 us -> 75.7 us  [local(): its = lax.ppermute(mine, 'groups', [(i, i ^ 1) for i in range(groups)])]
    pallas_call x1, Pallas kernels: 214 us -> 142 us  [near(): pl.pallas_call(functools.partial(near_kernel, n), grid=(heads,), out_shap...]
    all_gather x1, waiting for transfers between devices: 31.6 us -> 0.02 us  [local(): lax.all_gather(lax.dynamic_slice_in_dim(out_weight, side * piece, piece,...]
  transfers between devices with their start and end apart: 3 -> 3, of which waited for: 1 -> 1; matrix products, arithmetic and copies ran while one was open for 2% -> 2% of each run, Pallas kernels for 80% -> 64%
where the time goes in v4:
time: 320 us; the launch traced here: 316 us
  Pallas kernels  217 us (68%)
  waiting for transfers between devices  75.8 us (24%)
  between operations  13.5 us (4%)
  local copies, waits for them, and re-layouts  6.91 us (2%)
    pallas_call x1, Pallas kernels, near(): pl.pallas_call(functools.partial(near_kernel, n), grid=(heads,), out_shap...  142 us
    ppermute x1, waiting for transfers between devices, local(): its = lax.ppermute(mine, 'groups', [(i, i ^ 1) for i in range(groups)])  75.7 us
    pallas_call x1, Pallas kernels, far(): pl.pallas_call(functools.partial(far_kernel, picks, list_len), grid=(widt...  29.7 us
    pallas_call x3, Pallas kernels, project(): pl.pallas_call(project_kernel, out_shape=jax.ShapeDtypeStruct((tokens, wh...  26.6 us
    pallas_call x1, Pallas kernels, pick_blocks(): pl.pallas_call(pick_kernel, out_shape=jax.ShapeDtypeStruct((n, 2, picks)...  19 us
  transfers between devices with their start and end apart: 3, of which 1 were waited for; matrix products, arithmetic and copies ran while one was open for 2% of the time, Pallas kernels for 64%

profile of v4, /device:TPU:13, one launch (start us, length us, event | category | flops | bytes accessed | tf_op | source)
XLA Modules:
  0.0 316.3 jit_solution(2115804992133528867)
XLA Ops:
  6.5 0.0 all-gather.3.cloned.1.call-start
  6.5 1.7 constant_dynamic-slice_fusion
  8.3 0.0 all-gather.3.cloned.1.call-update
  8.3 0.0 all-gather.5.cloned.1.call-start
  8.4 0.8 fusion.5
  9.2 0.1 broadcast_bitcast_fusion.1
  9.3 0.8 copy.12
  10.1 0.1 reshape.89
  10.2 0.4 convert_reduce_fusion
  10.5 2.2 slice.3
  12.8 0.6 copy.19
  13.4 0.1 select_reduce_fusion
  13.5 0.1 copy.13
  13.6 0.7 reshape.93.wanted
  14.2 19.0 %pick.1.send = bf16[16,2,2,16,2560]{4,3,2,1,0:T(8,128)(2,1)} custom-call(s32[32]{0:T(128)} %reshape.93.wanted, bf16[48,16,2560]{2,1,0:T(8,128)(2,1)} %pk.1, bf16[48,16,2560]{2,1,0:T(8,128)(2,1)} %pv.1), custom_call_target="tpu_custom_call" | custom-call | tf_op jit(solution)/shard_map/pick/pallas_call | solution.py:44
  33.3 141.5 %near.1 = (f32[512,2560]{1,0:T(8,128)}, f32[512,2560]{1,0:T(8,128)}, f32[512,2560]{1,0:T(8,128)}, bf16[16,2,2,16,2560]{4,3,2,1,0:T(8,128)(2,1)}, bf16[2,512,2560]{2,1,0:T(8,128)(2,1)}) custom-call(bf16[512,2560]{1,0:T(8,128)(2,1)} %q.3, bf16[512,2560]{1,0:T(8,128)(2,1)} %ck_all.1, bf16[512,2560]{1,0:T(8,128)(2,1)} %cv_all.1, bf16[768,2560]{1,0:T(8,128)(2,1)} %bitcast.20, ...), custom_call_target="tpu_custom_call" | custom-call | flops 100663296000 | bytes 52428800 | tf_op jit(solution)/shard_map/near/pallas_call | solution.py:146
  174.8 0.0 all-gather.3.cloned.1.call-done.weight
  174.8 0.0 all-gather.5.cloned.1.call-update
  174.8 1.3 collective-permute-start
  176.1 0.1 broadcast_bitcast_fusion
  176.2 0.6 copy.18
  176.8 0.2 convert_reduce_fusion.1
  177.0 0.5 multiply_add_fusion.place
  177.5 29.7 %far.1.attended = bf16[512,2560]{1,0:T(8,128)(2,1)} custom-call(s32[32]{0:T(128)} %multiply_add_fusion.place, bf16[512,2560]{1,0:T(8,128)(2,1)} %q.3, bf16[2,512,2560]{2,1,0:T(8,128)(2,1)} %get-tuple-element.13.part, bf16[16,2,2,16,2560]{4,3,2,1,0:T(8,128)(2,1)} %get-tuple-element.15.got, f32[4,512]{1,0:T(4,128)} %bitcast.22, ...), custom_call_target="tpu_custom_call" | custom-call | flops 8053063680 | bytes 39321600 | tf_op jit(solution)/shard_map/far/pallas_call | solution.py:215
  207.2 6.4 %project.3.rest_0_ = bf16[512,5120]{1,0:T(8,128)(2,1)} custom-call(s32[1]{0:T(128)} %bitcast.6.first, bf16[512,2560]{1,0:T(8,128)(2,1)} %far.1.attended, bf16[2560,1024]{1,0:T(8,128)(2,1)} %all-gather.3.cloned.1.call-done.weight), custom_call_target="tpu_custom_call" | custom-call | flops 2684354560 | bytes 8912896 | tf_op jit(solution)/shard_map/project/pallas_call | solution.py:271
  213.6 75.7 %collective-permute-done.weight = bf16[2560,1024]{1,0:T(8,128)(2,1)} collective-permute-done((bf16[2560,1024]{1,0:T(8,128)(2,1)}, bf16[2560,1024]{1,0:T(8,128)(2,1)}, u32[]{:S(2)}, u32[]{:S(2)}) %collective-permute-start) | collective-permute-done | bytes 5242912 | tf_op jit(solution)/shard_map/ppermute | solution.py:320
  289.4 6.6 %project.4.rest_0_ = bf16[512,5120]{1,0:T(8,128)(2,1)} custom-call(s32[1]{0:T(128)} %bitcast.5.first, bf16[512,2560]{1,0:T(8,128)(2,1)} %far.1.attended, bf16[2560,1024]{1,0:T(8,128)(2,1)} %collective-permute-done.weight, bf16[512,5120]{1,0:T(8,128)(2,1)} %project.3.rest_0_), custom_call_target="tpu_custom_call", output_to_operand_aliasing={{}: (3, {})} | custom-call | flops 2684354560 | bytes 8912896 | tf_op jit(solution)/shard_map/project/pallas_call | solution.py:271
  296.0 0.0 all-gather.5.cloned.1.call-done.weight
  296.0 13.5 %project.5 = bf16[512,5120]{1,0:T(8,128)(2,1)} custom-call(s32[1]{0:T(128)} %constant.29.clone.1.first, bf16[512,2560]{1,0:T(8,128)(2,1)} %far.1.attended, bf16[2560,3072]{1,0:T(8,128)(2,1)} %all-gather.5.cloned.1.call-done.weight, bf16[512,5120]{1,0:T(8,128)(2,1)} %project.4.rest_0_), custom_call_target="tpu_custom_call", output_to_operand_aliasing={{}: (3, {})} | custom-call | flops 8053063680 | bytes 21495808 | tf_op jit(solution)/shard_map/project/pallas_call | solution.py:271
  (5 shorter events, 0.1 us)
Async XLA Ops:
  6.5 168.3 %all-gather.3.cloned.1.call-start = ((), (), s32[]{:S(2)}) async-start(), calls=%async_computation | async-start | bytes 5570560 | tf_op jit(solution)/shard_map/all_gather | solution.py:306
  8.3 287.7 %all-gather.5.cloned.1.call-start = ((), (), s32[]{:S(2)}) async-start(), calls=%async_computation.1 | async-start | bytes 16711680 | tf_op jit(solution)/shard_map/all_gather | solution.py:319
  174.8 114.5 %collective-permute-start = (bf16[2560,1024]{1,0:T(8,128)(2,1)}, bf16[2560,1024]{1,0:T(8,128)(2,1)}, u32[]{:S(2)}, u32[]{:S(2)}) collective-permute-start(bf16[2560,1024]{1,0:T(8,128)(2,1)} %all-gather.3.cloned.1.call-done.weight), channel_id=1, source_target_pairs={{0,16},{16,0},{1,17},{17,1},{2,18},{18,2},{3,19},{19,3},{4,20},{20... | collective-permute-start | bytes 15728648 | tf_op jit(solution)/shard_map/ppermute | solution.py:320
Sparse Core Ops, SparseCore 0:
  9.6 137.6 all-gather.2
  175.0 118.2 all-gather.4
